TPU v7x, 512 devices: a whole 4x4x16 slice. The times are simulated.
512 devices in a mesh: grp: 16 (over z), tile: 8 (over x_hi, y), arch: 4 (over x_lo, core).
Axes of the slice: x: 4 (x_hi: 2, x_lo: 2; x = x_hi * 2 + x_lo), y: 4, z: 16, core: 2. Of those that a mesh axis runs over, the one named last changes fastest.
Arguments:
- query_grads: bfloat16 [4, 1536, 4096], P('arch', 'tile', 'grp'), may hold values from -6 to 6
- input_basis: bfloat16 [4096, 4096], P(None, 'grp'), may hold values from -0.09375 to 0.09375
- output_basis: bfloat16 [1536, 1536], P(None, 'tile'), may hold values from -0.15625 to 0.15625
- eigenvalues: float32 [1536, 4096], P('tile', 'grp'), may hold values from 0.1 to 10
- activations: bfloat16 [1024, 4096], P('arch', 'grp'), may hold values from -6 to 6
- gradients: bfloat16 [1024, 1536], P('arch', 'tile'), may hold values from -0.0099487305 to 0.0099487305
- seq_lengths: int32 [4, 8], P('arch'), may hold values from 1 to 128, 256 in all within a row
Outputs:
- preconditioned: bfloat16 [4, 4096, 1536], P('arch', 'grp', 'tile')
- sequence_scores: float32 [4, 32], P(None, 'arch')
Inputs may be any that keep to these rules, and one draw needn't show every extreme that they name: Each row of seq_lengths sums to 256, and its largest entry is exactly 128.
All inputs are finite; a program needn't handle non-finite values.
Results may differ from a plain program's by a relative error of at most 0.013.
Values may be sent and summed in bfloat16 or wider, within the bound.
A program may use at most 64 MiB of HBM per device.

v0:
```python
import jax
import jax.numpy as jnp
from jax import lax
from jax.sharding import PartitionSpec as P

damping = 0.01


def contract_first(left_side, right_side):
    return lax.dot_general(
        left_side, right_side, (((0,), (0,)), ((), ())), preferred_element_type=jnp.float32
    )


def contract_last(left_side, right_side):
    return lax.dot_general(
        left_side, right_side, (((1,), (1,)), ((), ())), preferred_element_type=jnp.float32
    )


def per_device(
    query_grads, input_basis, output_basis, eigenvalues, activations, gradients, seq_lengths
):
    local_query = query_grads[0]
    feat_rows = local_query.shape[0]
    input_cols = local_query.shape[1]
    basis_part = input_basis
    rotated_in = jnp.dot(
        lax.all_gather(local_query, "grp", axis=1, tiled=True),
        basis_part,
        preferred_element_type=jnp.float32,
    ).astype(jnp.bfloat16)
    basis_part = output_basis
    rotated = contract_first(basis_part, lax.all_gather(rotated_in, "tile", axis=0, tiled=True))
    scaled = (rotated / (eigenvalues + damping)).astype(jnp.bfloat16)
    basis_part = output_basis
    restored = lax.psum_scatter(
        jnp.dot(basis_part, scaled, preferred_element_type=jnp.float32).astype(jnp.bfloat16),
        "tile",
        scatter_dimension=0,
        tiled=True,
    )
    basis_part = input_basis
    summed = lax.psum_scatter(
        contract_last(basis_part, restored), "grp", scatter_dimension=0, tiled=True
    )
    preconditioned = summed.astype(jnp.bfloat16)
    all_queries = lax.all_gather(preconditioned[None], "arch", axis=0, tiled=True)
    query_count = all_queries.shape[0]
    stacked = jnp.transpose(all_queries, (1, 0, 2)).reshape(input_cols, query_count * feat_rows)
    projected = jnp.dot(activations, stacked, preferred_element_type=jnp.float32)
    projected = projected.reshape(activations.shape[0], query_count, feat_rows)
    partial_scores = jnp.sum(projected * gradients.astype(jnp.float32)[:, None, :], axis=2).T
    lengths = seq_lengths[0]
    ends = jnp.cumsum(lengths)
    starts = ends - lengths
    position = jnp.arange(activations.shape[0], dtype=jnp.int32)
    member = ((position[None, :] >= starts[:, None]) & (position[None, :] < ends[:, None])).astype(
        jnp.float32
    )
    seq_sizes = lengths.astype(jnp.float32)
    token_scores = lax.psum(partial_scores, ("grp", "tile"))
    totals = jnp.dot(token_scores, member.T, precision=lax.Precision.HIGHEST)
    sequence_scores = totals / seq_sizes[None, :]
    return (preconditioned[None], sequence_scores)


def solution(mesh):
    return jax.shard_map(
        per_device,
        mesh=mesh,
        in_specs=(
            P("arch", "tile", "grp"),
            P(None, "grp"),
            P(None, "tile"),
            P("tile", "grp"),
            P("arch", "grp"),
            P("arch", "tile"),
            P("arch", None),
        ),
        out_specs=(P("arch", "grp", "tile"), P(None, "arch")),
        check_vma=False,
    )
```

profile of v0, /device:TPU:2, one launch (start us, length us, event | category | flops | bytes accessed | tf_op | source)
XLA Modules:
  0.0 666.5 jit_solution(9814027762734079321)
XLA Ops:
  7.2 0.0 copy-start
  7.2 0.0 all-gather.4.cloned.1.call-start
  7.2 0.7 all-gather.4.cloned.1.call-update
  7.9 0.0 copy-start.1
  7.9 0.0 reduce-scatter.7.cloned.1.call-start
  8.0 82.4 %all-gather.4.cloned.1.call-done = bf16[1,192,4096]{2,1,0:T(8,128)(2,1)} async-done(((bf16[1,192,256]{2,1,0:T(8,128)(2,1)}), bf16[1,192,4096]{2,1,0:T(8,128)(2,1)}) %all-gather.4.cloned.1.call-update) | async-done | bytes 1572880 | tf_op jit(solution)/shard_map/all_gather | solution.py:29
  90.3 0.0 copy-done
  90.3 2.0 fusion.5
  92.3 35.8 %all_gather.10 = bf16[1536,256]{1,0:T(8,128)(2,1)S(1)} all-gather(bf16[192,256]{1,0:T(8,128)(2,1)S(1)} %fusion.5), channel_id=1, replica_groups=mesh['grp'=16,'tile'=8,'arch'=4] {'tile'}, dimensions={0}, use_global_device_ids=true | all-gather | bytes 884736 | tf_op jit(solution)/shard_map/all_gather | solution.py:34
  128.2 0.0 copy-done.1
  128.2 2.8 fusion
  131.0 2.3 copy.11
  133.3 0.0 reduce-scatter.7.cloned.1.call-update
  133.3 0.0 reduce-scatter.5.cloned.1.call-start
  133.3 81.0 %reduce-scatter.7.cloned.1.call-done = bf16[192,256]{1,0:T(8,128)(2,1)} async-done(((bf16[1536,256]{1,0:T(8,128)(2,1)}), bf16[192,256]{1,0:T(8,128)(2,1)}) %reduce-scatter.7.cloned.1.call-update) | async-done | bytes 98320
  214.3 3.4 convolution_bitcast_fusion
  217.7 0.0 copy-start.4
  217.7 0.0 copy-start.5
  217.7 0.0 copy-start.3
  217.7 0.0 reduce-scatter.5.cloned.1.call-update
  217.8 0.9 copy-done.4
  218.6 0.0 copy-done.5
  218.6 0.2 reduce-window.7
  218.8 75.6 %reduce-scatter.5.cloned.1.call-done = f32[256,192]{0,1:T(8,128)} async-done(((f32[4096,192]{0,1:T(8,128)}), f32[256,192]{0,1:T(8,128)}) %reduce-scatter.5.cloned.1.call-update) | async-done | bytes 196624 | tf_op jit(solution)/shard_map/reduce_scatter | solution.py:44
  294.4 0.0 copy-start.2
  294.4 1.0 convert_element_type.27
  295.4 6.1 all-gather.1
  301.6 0.0 copy-done.3
  301.6 0.3 fusion.15
  301.9 0.1 multiply_reduce_fusion
  302.0 356.6 %psum.7 = f32[4,256]{1,0:T(4,128)S(1)} all-reduce(f32[4,256]{1,0:T(4,128)S(1)} %bitcast.50), channel_id=1, replica_groups=mesh['grp'=16,'tile'=8,'arch'=4] {'grp','tile'}, use_global_device_ids=true, to_apply=%region_3.0 | all-reduce | flops 1024 | bytes 8192 | tf_op jit(solution)/shard_map/psum | solution.py:62
  658.6 0.8 convolution_divide_fusion
  659.4 0.0 copy-done.2
  659.4 0.7 convert_bitcast_fusion.1
  (4 shorter events, 0.0 us)
Async XLA Ops:
  7.2 83.2 %copy-start = (bf16[4096,256]{1,0:T(8,128)(2,1)S(1)}, bf16[4096,256]{1,0:T(8,128)(2,1)}, u32[]{:S(2)}) copy-start(bf16[4096,256]{1,0:T(8,128)(2,1)} %param.8) | copy-start | bytes 6291460
  7.2 83.2 %all-gather.4.cloned.1.call-start = ((), (), s32[]{:S(2)}) async-start(), calls=%async_computation.3 | async-start | bytes 1671168 | tf_op jit(solution)/shard_map/all_gather | solution.py:29
  7.9 120.3 %copy-start.1 = (bf16[1536,192]{0,1:T(8,128)(2,1)S(1)}, bf16[1536,192]{0,1:T(8,128)(2,1)}, u32[]{:S(2)}) copy-start(bf16[1536,192]{0,1:T(8,128)(2,1)} %param.9) | copy-start | bytes 1769476
  7.9 206.4 %reduce-scatter.7.cloned.1.call-start = ((), (), s32[]{:S(2)}) async-start(), calls=%async_computation.4 | async-start | bytes 884736
  133.3 161.1 %reduce-scatter.5.cloned.1.call-start = ((), (), s32[]{:S(2)}) async-start(), calls=%async_computation.2 | async-start | bytes 3342336 | tf_op jit(solution)/shard_map/reduce_scatter | solution.py:44
  217.7 0.9 copy-start.4
  217.7 0.9 copy-start.5
  217.7 83.9 %copy-start.3 = (bf16[256,256]{1,0:T(8,128)(2,1)S(1)}, bf16[256,256]{1,0:T(8,128)(2,1)}, u32[]{:S(2)}) copy-start(bf16[256,256]{1,0:T(8,128)(2,1)} %param.11) | copy-start | bytes 393220
  294.4 364.9 %copy-start.2 = (f32[256,192]{0,1:T(8,128)S(1)}, f32[256,192]{0,1:T(8,128)}, u32[]{:S(2)}) copy-start(f32[256,192]{0,1:T(8,128)} %reduce-scatter.5.cloned.1.call-done) | copy-start | bytes 589828
Sparse Core Ops, SparseCore 0:
  10.0 80.2 all-gather.3
  133.4 80.8 reduce-scatter.6
  217.9 76.5 reduce-scatter.4
where the time goes:
time: 667 us
  blocking collectives  399 us (60%)
  waiting for transfers between devices  240 us (36%)
  between operations  13.8 us (2%)
  matrix products  9.26 us (1%)
    psum x1, blocking collectives, per_device(): token_scores = lax.psum(partial_scores, ('grp', 'tile'))  357 us
    all_gather x1, waiting for transfers between devices, per_device(): lax.all_gather(local_query, 'grp', axis=1, tiled=True)  82.4 us
    unnamed x4, waiting for transfers between devices  81.7 us
    reduce_scatter x1, waiting for transfers between devices, per_device(): lax.psum_scatter(contract_last(basis_part, restored), 'grp', scatter_dime...  75.6 us
    all_gather x1, blocking collectives, per_device(): lax.all_gather(rotated_in, 'tile', axis=0, tiled=True)  35.8 us
  transfers between devices with their start and end apart: 3, of which 3 were waited for; matrix products, arithmetic and copies ran while one was open for 0% of the time, Pallas kernels for 0%

commit v1 on v0

--- a/solution.py
+++ b/solution.py
@@ -4,6 +4,18 @@
 from jax.sharding import PartitionSpec as P
 
 damping = 0.01
+
+
+def collect(value, axis, dim):
+    ways, here, hop = (lax.axis_size(axis), lax.axis_index(axis), value.shape[dim])
+    line, have = (value, 1)
+    while have < ways:
+        line = jnp.concatenate(
+            [line, lax.ppermute(line, axis, [(d, (d - have) % ways) for d in range(ways)])],
+            axis=dim,
+        )
+        have = 2 * have
+    return jnp.roll(line, here * hop, axis=dim)
 
 
 def contract_first(left_side, right_side):
@@ -26,9 +38,7 @@
     input_cols = local_query.shape[1]
     basis_part = input_basis
     rotated_in = jnp.dot(
-        lax.all_gather(local_query, "grp", axis=1, tiled=True),
-        basis_part,
-        preferred_element_type=jnp.float32,
+        collect(local_query, "grp", 1), basis_part, preferred_element_type=jnp.float32
     ).astype(jnp.bfloat16)
     basis_part = output_basis
     rotated = contract_first(basis_part, lax.all_gather(rotated_in, "tile", axis=0, tiled=True))

time: 667 us -> 723 us (1.084)
  starting transfers between devices: 0.12 us -> 31.6 us
  waiting for transfers between devices: 240 us -> 261 us
    all_gather x1 -> x0, waiting for transfers between devices: 82.4 us -> none  [per_device(): lax.all_gather(local_query, 'grp', axis=1, tiled=True)]
    ppermute x0 -> x4, waiting for transfers between devices: none -> 70.1 us  [collect(): lax.ppermute(line, axis, [(d, (d - have) % ways) for d in range(ways)])]
    unnamed x4 -> x3, waiting for transfers between devices: 81.7 us -> 114 us
    ppermute x0 -> x4, starting transfers between devices: none -> 31.5 us  [collect(): lax.ppermute(line, axis, [(d, (d - have) % ways) for d in range(ways)])]
  transfers between devices with their start and end apart: 3 -> 6, of which waited for: 3 -> 6; matrix products, arithmetic and copies ran while one was open for 0% -> 0% of each run, Pallas kernels for 0% -> 0%
where the time goes in v1:
time: 723 us
  blocking collectives  398 us (55%)
  waiting for transfers between devices  261 us (36%)
  starting transfers between devices  31.6 us (4%)
  between operations  14.3 us (2%)
  matrix products  7.84 us (1%)
    psum x1, blocking collectives, per_device(): token_scores = lax.psum(partial_scores, ('grp', 'tile'))  357 us
    unnamed x3, waiting for transfers between devices  114 us
    reduce_scatter x1, waiting for transfers between devices, per_device(): lax.psum_scatter(contract_last(basis_part, restored), 'grp', scatter_dime...  76.5 us
    ppermute x4, waiting for transfers between devices, collect(): lax.ppermute(line, axis, [(d, (d - have) % ways) for d in range(ways)])  70.1 us
    all_gather x1, blocking collectives, per_device(): lax.all_gather(rotated_in, 'tile', axis=0, tiled=True)  35.6 us
    ppermute x4, starting transfers between devices, collect(): lax.ppermute(line, axis, [(d, (d - have) % ways) for d in range(ways)])  31.5 us
  transfers between devices with their start and end apart: 6, of which 6 were waited for; matrix products, arithmetic and copies ran while one was open for 0% of the time, Pallas kernels for 0%

profile of v1, /device:TPU:2, one launch (start us, length us, event | category | flops | bytes accessed | tf_op | source)
XLA Modules:
  0.0 722.8 jit_solution(314028421581750892)
XLA Ops:
  7.2 0.0 copy-start
  7.2 0.0 reduce-scatter.7.cloned.1.call-start
  7.2 11.5 %collective-permute-start = (bf16[192,256]{1,0:T(8,128)(2,1)}, bf16[192,256]{1,0:T(8,128)(2,1)S(1)}, u32[]{:S(2)}, u32[]{:S(2)}) collective-permute-start(bf16[192,256]{1,0:T(8,128)(2,1)} %bitcast.46), channel_id=1, source_target_pairs={{0,480},{32,0},{64,32},{96,64},{128,96},{160,128},{192,160},{224,1... | collective-permute-start | bytes 294920 | tf_op jit(solution)/shard_map/ppermute | solution.py:14
  18.8 2.5 collective-permute-done
  21.3 0.0 copy-start.2
  21.3 0.9 pad_maximum_fusion.2
  22.2 4.7 collective-permute-start.1
  26.9 6.6 collective-permute-done.1
  33.4 0.9 pad_maximum_fusion.1
  34.4 6.6 collective-permute-start.2
  41.0 24.8 %collective-permute-done.2 = bf16[192,1024]{1,0:T(8,128)(2,1)S(1)} collective-permute-done((bf16[192,1024]{1,0:T(8,128)(2,1)S(1)}, bf16[192,1024]{1,0:T(8,128)(2,1)S(1)}, u32[]{:S(2)}, u32[]{:S(2)}) %collective-permute-start.2) | collective-permute-done | bytes 393248 | tf_op jit(solution)/shard_map/ppermute | solution.py:14
  65.8 0.0 copy-done.2
  65.8 1.9 pad_maximum_fusion
  67.6 8.7 %collective-permute-start.3 = (bf16[192,2048]{1,0:T(8,128)(2,1)}, bf16[192,2048]{1,0:T(8,128)(2,1)S(1)}, u32[]{:S(2)}, u32[]{:S(2)}) collective-permute-start(bf16[192,2048]{1,0:T(8,128)(2,1)} %pad_maximum_fusion), channel_id=1, source_target_pairs={{0,256},{32,288},{64,320},{96,352},{128,384},{160,416},{192,448},{... | collective-permute-start | bytes 2359304 | tf_op jit(solution)/shard_map/ppermute | solution.py:14
  76.4 0.0 copy-start.1
  76.4 0.0 copy-start.3
  76.4 1.0 constant_dynamic-update-slice_fusion.9
  77.3 0.9 constant_dynamic-update-slice_fusion.8
  78.3 36.3 %collective-permute-done.3 = bf16[192,2048]{1,0:T(8,128)(2,1)S(1)} collective-permute-done((bf16[192,2048]{1,0:T(8,128)(2,1)}, bf16[192,2048]{1,0:T(8,128)(2,1)S(1)}, u32[]{:S(2)}, u32[]{:S(2)}) %collective-permute-start.3) | collective-permute-done | bytes 786464 | tf_op jit(solution)/shard_map/ppermute | solution.py:14
  114.6 0.1 constant_dynamic-update-slice_fusion.5
  114.7 0.0 copy-done.1
  114.7 0.0 copy-done.3
  114.8 0.1 constant_dynamic-update-slice_fusion
  114.9 0.0 copy-done
  114.9 0.0 copy-start.4
  114.9 0.6 fusion.5
  115.5 35.6 %all_gather.6 = bf16[1536,256]{1,0:T(8,128)(2,1)S(1)} all-gather(bf16[192,256]{1,0:T(8,128)(2,1)S(1)} %fusion.5), channel_id=1, replica_groups=mesh['grp'=16,'tile'=8,'arch'=4] {'tile'}, dimensions={0}, use_global_device_ids=true | all-gather | bytes 884736 | tf_op jit(solution)/shard_map/all_gather | solution.py:44
  151.1 0.0 copy-done.4
  151.1 2.8 fusion
  153.9 2.3 copy.11
  156.2 0.0 reduce-scatter.7.cloned.1.call-update
  156.2 0.0 copy-start.7
  156.3 0.0 copy-start.8
  156.3 0.0 reduce-scatter.5.cloned.1.call-start
  156.3 114.0 %reduce-scatter.7.cloned.1.call-done = bf16[192,256]{1,0:T(8,128)(2,1)} async-done(((bf16[1536,256]{1,0:T(8,128)(2,1)}), bf16[192,256]{1,0:T(8,128)(2,1)}) %reduce-scatter.7.cloned.1.call-update) | async-done | bytes 98320
  270.3 3.4 convolution_bitcast_fusion
  273.7 0.0 copy-start.6
  273.7 0.0 reduce-scatter.5.cloned.1.call-update
  273.7 0.0 copy-done.7
  273.7 0.0 copy-done.8
  273.7 0.2 reduce-window.7
  273.9 76.5 %reduce-scatter.5.cloned.1.call-done = f32[256,192]{0,1:T(8,128)} async-done(((f32[4096,192]{0,1:T(8,128)}), f32[256,192]{0,1:T(8,128)}) %reduce-scatter.5.cloned.1.call-update) | async-done | bytes 196624 | tf_op jit(solution)/shard_map/reduce_scatter | solution.py:54
  350.4 0.0 copy-start.5
  350.4 1.0 convert_element_type.27
  351.4 6.1 all-gather
  357.6 0.0 copy-done.6
  357.6 0.3 fusion.16
  357.9 0.1 multiply_reduce_fusion
  358.0 356.5 %psum.7 = f32[4,256]{1,0:T(4,128)S(1)} all-reduce(f32[4,256]{1,0:T(4,128)S(1)} %bitcast.52), channel_id=1, replica_groups=mesh['grp'=16,'tile'=8,'arch'=4] {'grp','tile'}, use_global_device_ids=true, to_apply=%region_3.4 | all-reduce | flops 1024 | bytes 8192 | tf_op jit(solution)/shard_map/psum | solution.py:72
  714.5 0.8 convolution_divide_fusion
  715.3 0.0 copy-done.5
  715.3 0.7 convert_bitcast_fusion.1
  (10 shorter events, 0.2 us)
Async XLA Ops:
  7.2 107.7 %copy-start = (bf16[4096,256]{1,0:T(8,128)(2,1)S(1)}, bf16[4096,256]{1,0:T(8,128)(2,1)}, u32[]{:S(2)}) copy-start(bf16[4096,256]{1,0:T(8,128)(2,1)} %param.8) | copy-start | bytes 6291460
  7.2 263.1 %reduce-scatter.7.cloned.1.call-start = ((), (), s32[]{:S(2)}) async-start(), calls=%async_computation.3 | async-start | bytes 884736
  7.2 14.1 %collective-permute-start = (bf16[192,256]{1,0:T(8,128)(2,1)}, bf16[192,256]{1,0:T(8,128)(2,1)S(1)}, u32[]{:S(2)}, u32[]{:S(2)}) collective-permute-start(bf16[192,256]{1,0:T(8,128)(2,1)} %bitcast.46), channel_id=1, source_target_pairs={{0,480},{32,0},{64,32},{96,64},{128,96},{160,128},{192,160},{224,1... | collective-permute-start | bytes 294920 | tf_op jit(solution)/shard_map/ppermute | solution.py:14
  21.3 44.5 %copy-start.2 = (bf16[192,256]{1,0:T(8,128)(2,1)}, bf16[192,256]{1,0:T(8,128)(2,1)S(1)}, u32[]{:S(2)}) copy-start(bf16[192,256]{1,0:T(8,128)(2,1)S(1)} %collective-permute-done) | copy-start | bytes 294916
  22.2 11.2 %collective-permute-start.1 = (bf16[192,512]{1,0:T(8,128)(2,1)S(1)}, bf16[192,512]{1,0:T(8,128)(2,1)S(1)}, u32[]{:S(2)}, u32[]{:S(2)}) collective-permute-start(bf16[192,512]{1,0:T(8,128)(2,1)S(1)} %pad_maximum_fusion.2), channel_id=1, source_target_pairs={{0,448},{32,480},{64,0},{96,32},{128,64},{160,96},{192,128},{224,1... | collective-permute-start | bytes 589832 | tf_op jit(solution)/shard_map/ppermute | solution.py:14
  34.4 31.4 %collective-permute-start.2 = (bf16[192,1024]{1,0:T(8,128)(2,1)S(1)}, bf16[192,1024]{1,0:T(8,128)(2,1)S(1)}, u32[]{:S(2)}, u32[]{:S(2)}) collective-permute-start(bf16[192,1024]{1,0:T(8,128)(2,1)S(1)} %pad_maximum_fusion.1), channel_id=1, source_target_pairs={{0,384},{32,416},{64,448},{96,480},{128,0},{160,32},{192,64},{224,... | collective-permute-start | bytes 1179656 | tf_op jit(solution)/shard_map/ppermute | solution.py:14
  67.6 47.0 %collective-permute-start.3 = (bf16[192,2048]{1,0:T(8,128)(2,1)}, bf16[192,2048]{1,0:T(8,128)(2,1)S(1)}, u32[]{:S(2)}, u32[]{:S(2)}) collective-permute-start(bf16[192,2048]{1,0:T(8,128)(2,1)} %pad_maximum_fusion), channel_id=1, source_target_pairs={{0,256},{32,288},{64,320},{96,352},{128,384},{160,416},{192,448},{... | collective-permute-start | bytes 2359304 | tf_op jit(solution)/shard_map/ppermute | solution.py:14
  76.4 38.3 %copy-start.1 = (bf16[1,192,256]{2,1,0:T(8,128)(2,1)S(1)}, bf16[1,192,256]{2,1,0:T(8,128)(2,1)}, u32[]{:S(2)}) copy-start(bf16[1,192,256]{2,1,0:T(8,128)(2,1)} %param.7) | copy-start | bytes 294916
  76.4 38.3 %copy-start.3 = (bf16[192,256]{1,0:T(8,128)(2,1)S(1)}, bf16[192,256]{1,0:T(8,128)(2,1)}, u32[]{:S(2)}) copy-start(bf16[192,256]{1,0:T(8,128)(2,1)} %copy-done.2) | copy-start | bytes 294916
  114.9 36.2 %copy-start.4 = (bf16[1536,192]{0,1:T(8,128)(2,1)S(1)}, bf16[1536,192]{0,1:T(8,128)(2,1)}, u32[]{:S(2)}) copy-start(bf16[1536,192]{0,1:T(8,128)(2,1)} %param.9) | copy-start | bytes 1769476
  156.2 117.4 %copy-start.7 = (bf16[256,192]{0,1:T(8,128)(2,1)S(1)}, bf16[256,192]{0,1:T(8,128)(2,1)}, u32[]{:S(2)}) copy-start(bf16[256,192]{0,1:T(8,128)(2,1)} %param.12) | copy-start | bytes 294916
  156.3 117.5 %copy-start.8 = (s32[1,8]{1,0:T(1,128)S(1)}, s32[1,8]{1,0:T(1,128)}, u32[]{:S(2)}) copy-start(s32[1,8]{1,0:T(1,128)} %param.13) | copy-start | bytes 100
  156.3 194.1 %reduce-scatter.5.cloned.1.call-start = ((), (), s32[]{:S(2)}) async-start(), calls=%async_computation.2 | async-start | bytes 3342336 | tf_op jit(solution)/shard_map/reduce_scatter | solution.py:54
  273.7 83.9 %copy-start.6 = (bf16[256,256]{1,0:T(8,128)(2,1)S(1)}, bf16[256,256]{1,0:T(8,128)(2,1)}, u32[]{:S(2)}) copy-start(bf16[256,256]{1,0:T(8,128)(2,1)} %param.11) | copy-start | bytes 393220
  350.4 364.9 %copy-start.5 = (f32[256,192]{0,1:T(8,128)S(1)}, f32[256,192]{0,1:T(8,128)}, u32[]{:S(2)}) copy-start(f32[256,192]{0,1:T(8,128)} %reduce-scatter.5.cloned.1.call-done) | copy-start | bytes 589828
Sparse Core Ops, SparseCore 0:
  156.4 113.8 reduce-scatter.6
  273.8 76.5 reduce-scatter.4
